TPU v7x, 32 devices: a whole 2x2x4 slice. The times are simulated.
32 devices in a mesh: sec: 2 (over core), lat: 4 (over z), lon: 4 (over y, x).
Axes of the slice: x: 2, y: 2, z: 4, core: 2. Of those that a mesh axis runs over, the one named last changes fastest.
Arguments:
- adjoint: float32 [2, 4, 4, 128, 512], P('sec', None, None, 'lat', 'lon'), may hold values from -6 to 6
- diffusivity: float32 [2, 4, 128, 512], P('sec', None, 'lat', 'lon'), may hold values from 0.02 to 0.2
- velocity: float32 [2, 2, 4, 128, 512], P('sec', None, None, 'lat', 'lon'), may hold values from -0.4 to 0.4
- sensitivity: float32 [2, 4, 4], P('sec'), may hold values from -3 to 3
- sea_mask: int32 [2, 128, 512], P('sec', 'lat', 'lon'), may hold values 0 or 1
- coast_distance: int32 [2, 128, 512], P('sec', 'lat', 'lon'), may hold values from 0 to 31
- send_cells: int32 [2, 4, 12, 1024], P('sec', 'lat', 'lon'), may hold values from 0 to 4095
- recv_slots: int32 [2, 4, 128, 512], P('sec', None, 'lat', 'lon'), may hold values from 0 to 3071
- regrid_weight: float32 [2, 4, 128, 512], P('sec', None, 'lat', 'lon'), may hold values from 0.1 to 0.5
Outputs:
- adjoint_out: float32 [2, 4, 4, 128, 512], P('sec', None, None, 'lat', 'lon')
Inputs may be any that keep to these rules, and one draw needn't show every extreme that they name: `send_cells`: a cell number of the sending tile. `recv_slots`: an entry of the 3072 received entries, source tile major, west source first.
All inputs are finite; a program needn't handle non-finite values. No bound on the sum of `sea_mask` on one device may be relied on, other than what follows from the above.
Results may differ from a plain program's by a relative error of at most 0.0003.
Values sent between devices are 32-bit elements; how exact they have to be, the bound alone decides.
A program may use at most 64 MiB of HBM per device.

v0:
```python
import jax
import jax.numpy as jnp
from jax import lax
from jax.sharding import PartitionSpec as P

COMP = 4
TERMS = 4
STEPS = 2


def padded_2(block, sides, width, periodic):
    for axis, dim in sides:
        count = lax.axis_size(axis)
        forward = [(i, i + 1) for i in range(count - 1)]
        if periodic:
            forward.append((count - 1, 0))
        backward = [(target, source) for source, target in forward]
        low = lax.ppermute(
            lax.slice_in_dim(block, block.shape[dim] - width, None, axis=dim), axis, forward
        )
        high = lax.ppermute(lax.slice_in_dim(block, 0, width, axis=dim), axis, backward)
        block = jnp.concatenate([low, block, high], axis=dim)
    return block


def shifted(value, axis, steps):
    count = lax.axis_size(axis)
    pairs = [(source, (source + steps) % count) for source in range(count)]
    return lax.ppermute(value, axis, pairs)


def partner(block, axis, stride):
    count = lax.axis_size(axis)
    route = []
    for low in range(count):
        high = low | 1 << stride
        if high != low and high < count:
            route += [(low, high), (high, low)]
    return lax.ppermute(block, axis, route)


def widen_rims(array):
    across = padded_2(array, (("lon", 3),), 1, True)
    return padded_2(across, (("lat", 2),), 1, False)


def sweep_once(field, coef_padded):
    padded = widen_rims(field)
    diffused = coef_padded[0:1] * padded
    carried_x = coef_padded[1:2] * padded
    carried_y = coef_padded[2:3] * padded
    centre = diffused[..., 1:-1, 1:-1]
    laplace = (
        diffused[..., 2:, 1:-1]
        + diffused[..., :-2, 1:-1]
        + diffused[..., 1:-1, 2:]
        + diffused[..., 1:-1, :-2]
        - 4.0 * centre
    )
    advect = 0.5 * (carried_x[..., 1:-1, 2:] - carried_x[..., 1:-1, :-2]) + 0.5 * (
        carried_y[..., 2:, 1:-1] - carried_y[..., :-2, 1:-1]
    )
    return field + laplace + advect


def couple(field, sensitivity, weight_sea, send_list, slot_list, weight_list):
    surface = field[:, 0]
    fluxes = []
    for which in range(COMP):
        total = jnp.zeros(surface.shape[1:], jnp.float32)
        for other in range(COMP):
            total = total + sensitivity[which, other] * surface[other]
        fluxes.append(weight_sea * total)
    flux = jnp.stack(fluxes, axis=0).reshape(COMP, -1)
    peers = send_list.shape[0]
    packed = jnp.take(flux, send_list.reshape(-1), axis=1).reshape(COMP, peers, send_list.shape[1])
    arrived = []
    for offset in (1, -1):
        arrived.append(shifted(packed[:, 1 + offset], "lon", offset))
    routed = jnp.stack([arrived[0], packed[:, 1], arrived[1]], axis=1)
    received = partner(routed, "sec", 0).reshape(COMP, -1)
    cells = slot_list.shape[1]
    picked_all = jnp.take(received, slot_list.reshape(-1), axis=1).reshape(COMP, TERMS, cells)
    total = jnp.zeros((COMP, cells), jnp.float32)
    for which in range(TERMS):
        total = total + weight_list[which][None, :] * picked_all[:, which]
    return total.reshape(surface.shape)


def on_device(
    adjoint,
    diffusivity,
    velocity,
    sensitivity,
    sea_mask,
    coast_distance,
    send_cells,
    recv_slots,
    regrid_weight,
):
    field = adjoint[0]
    distance = coast_distance[0].astype(jnp.float32)
    blend = (distance + 1.0) / (distance + 9.0)
    weight_sea = sea_mask[0].astype(jnp.float32) * blend
    coefficients = jnp.concatenate([diffusivity[0][None], velocity[0]], axis=0)
    coef_padded = widen_rims(coefficients)
    send_list = send_cells[0, 0]
    slot_list = recv_slots[0].reshape(TERMS, -1)
    weight_list = regrid_weight[0].reshape(TERMS, -1)
    for step_index in range(STEPS):
        coupled = couple(field, sensitivity[0], weight_sea, send_list, slot_list, weight_list)
        field = sweep_once(field, coef_padded)
        field = field.at[:, 0].add(coupled)
    return field[None]


def solution(mesh):
    placed = (
        P("sec", None, None, "lat", "lon"),
        P("sec", None, "lat", "lon"),
        P("sec", None, None, "lat", "lon"),
        P("sec", None, None),
        P("sec", "lat", "lon"),
        P("sec", "lat", "lon"),
        P("sec", "lat", "lon", None),
        P("sec", None, "lat", "lon"),
        P("sec", None, "lat", "lon"),
    )
    return jax.shard_map(
        on_device,
        mesh=mesh,
        in_specs=placed,
        out_specs=P("sec", None, None, "lat", "lon"),
        check_vma=False,
    )
```

profile of v0, /device:TPU:0, one launch (start us, length us, event | category | flops | bytes accessed | tf_op | source)
XLA Modules:
  0.0 271.1 jit_solution(10875798243181095736)
XLA Ops:
  3.4 3.4 %bitcast_multiply_fusion.7 = (f32[1,32,128]{2,1,0:T(8,128)S(1)}, f32[1,32,128]{2,1,0:T(8,128)S(1)}) fusion(f32[4,4,32,128]{3,2,1,0:T(8,128)} %bitcast.99, f32[]{:T(128)} %bitcast.12, f32[]{:T(128)} %bitcast.11, f32[]{:T(128)} %bitcast.10, f32[]{:T(128)} %bitcast.9, s32[1,32,128]{2,1,0:T(8,128)} %param.22, s32[1,32,128]{2,1,0:T(8,128)} %param.21), kind=kLoop, calls=%fused_computation.69 | loop fusion | flops 57344 | bytes 131088 | tf_op jit(solution)/shard_map/mul | solution.py:73
  6.8 3.3 %bitcast_multiply_fusion.5 = f32[1,32,128]{2,1,0:T(8,128)S(1)} fusion(f32[1,32,128]{2,1,0:T(8,128)S(1)} %get-tuple-element.34, f32[4,4,32,128]{3,2,1,0:T(8,128)} %bitcast.100, f32[]{:T(128)} %bitcast.24, f32[]{:T(128)} %bitcast.23, f32[]{:T(128)} %bitcast.22, f32[]{:T(128)} %bitcast.21), kind=kLoop, calls=%fused_computation.67 | loop fusion | flops 32768 | bytes 98320 | tf_op jit(solution)/shard_map/mul | solution.py:73
  10.1 5.6 %bitcast_multiply_fusion.6 = (f32[1,32,128]{2,1,0:T(8,128)S(1)}, f32[1,32,128]{2,1,0:T(8,128)S(1)}) fusion(f32[1,32,128]{2,1,0:T(8,128)S(1)} %get-tuple-element.34, f32[4,4,32,128]{3,2,1,0:T(8,128)} %bitcast.101, f32[]{:T(128)} %bitcast.18, f32[]{:T(128)} %bitcast.17, f32[]{:T(128)} %bitcast.16, f32[]{:T(128)} %bitcast.15, f32[]{:T(128)} %bitcast.30, ...), kind=kLoop, calls=%fused_computation.68 | loop fusion | flops 65536 | bytes 114720 | tf_op jit(solution)/shard_map/mul | solution.py:73
  16.5 10.9 %gather_fusion = f32[3072,4]{1,0:T(8,128)} fusion(f32[4,4096]{0,1:T(8,128)S(1)} %copy.46, s32[3072]{0:T(1024)S(1)} %fusion.13), kind=kCustom, calls=%fused_computation.clone | custom fusion | bytes 110592 | tf_op jit(solution)/shard_map/jit(_take)/gather | solution.py:76
  27.4 2.7 broadcast_select_fusion.3
  30.4 3.0 %collective-permute-start.8 = (f32[4,1024]{1,0:T(4,128)S(1)}, f32[4,1024]{1,0:T(4,128)S(1)}, u32[]{:S(2)}, u32[]{:S(2)}) collective-permute-start(f32[4,1024]{1,0:T(4,128)S(1)} %bitcast.134), channel_id=1, source_target_pairs={{0,1},{1,2},{2,3},{3,0},{4,5},{5,6},{6,7},{7,4},{8,9},{9,10},{10,1... | collective-permute-start | bytes 49160 | tf_op jit(solution)/shard_map/ppermute | solution.py:29
  38.6 4.8 %collective-permute-done = f32[3,4,32,1]{3,2,1,0:T(8,128)S(1)} collective-permute-done((f32[3,4,32,1]{3,2,1,0:T(8,128)S(1)}, f32[3,4,32,1]{3,2,1,0:T(8,128)S(1)}, u32[]{:S(2)}, u32[]{:S(2)}) %collective-permute-start) | collective-permute-done | bytes 1568 | tf_op jit(solution)/shard_map/ppermute | solution.py:18
  44.6 3.6 %collective-permute-done.1 = f32[3,4,32,1]{3,2,1,0:T(8,128)S(1)} collective-permute-done((f32[3,4,32,1]{3,2,1,0:T(8,128)S(1)}, f32[3,4,32,1]{3,2,1,0:T(8,128)S(1)}, u32[]{:S(2)}, u32[]{:S(2)}) %collective-permute-start.1) | collective-permute-done | bytes 1568 | tf_op jit(solution)/shard_map/ppermute | solution.py:21
  48.4 3.5 %collective-permute-start.2 = (f32[3,4,1,130]{3,2,1,0:T(1,128)S(1)}, f32[3,4,1,130]{3,2,1,0:T(1,128)S(1)}, u32[]{:S(2)}, u32[]{:S(2)}) collective-permute-start(f32[3,4,1,130]{3,2,1,0:T(1,128)S(1)} %get-tuple-element.59), channel_id=1, source_target_pairs={{0,4},{4,8},{8,12},{1,5},{5,9},{9,13},{2,6},{6,10},{10,14},{3,7},{... | collective-permute-start | bytes 18728 | tf_op jit(solution)/shard_map/ppermute | solution.py:18
  54.6 3.1 %collective-permute-done.5 = f32[4,4,32,1]{3,2,1,0:T(8,128)S(1)} collective-permute-done((f32[4,4,32,1]{3,2,1,0:T(8,128)S(1)}, f32[4,4,32,1]{3,2,1,0:T(8,128)S(1)}, u32[]{:S(2)}, u32[]{:S(2)}) %collective-permute-start.5) | collective-permute-done | bytes 2080 | tf_op jit(solution)/shard_map/ppermute | solution.py:21
  57.9 3.5 %collective-permute-start.6 = (f32[4,4,1,130]{3,2,1,0:T(1,128)S(1)}, f32[4,4,1,130]{3,2,1,0:T(1,128)S(1)}, u32[]{:S(2)}, u32[]{:S(2)}) collective-permute-start(f32[4,4,1,130]{3,2,1,0:T(1,128)S(1)} %get-tuple-element.57), channel_id=1, source_target_pairs={{0,4},{4,8},{8,12},{1,5},{5,9},{9,13},{2,6},{6,10},{10,14},{3,7},{... | collective-permute-start | bytes 24968 | tf_op jit(solution)/shard_map/ppermute | solution.py:18
  63.0 4.0 %collective-permute-done.7 = f32[4,4,1,130]{3,2,1,0:T(1,128)S(1)} collective-permute-done((f32[4,4,1,130]{3,2,1,0:T(1,128)S(1)}, f32[4,4,1,130]{3,2,1,0:T(1,128)S(1)}, u32[]{:S(2)}, u32[]{:S(2)}) %collective-permute-start.7) | collective-permute-done | bytes 8352 | tf_op jit(solution)/shard_map/ppermute | solution.py:21
  69.2 54.8 %gather_fusion.1 = f32[16384,4]{1,0:T(8,128)} fusion(f32[4,3072]{0,1:T(8,128)S(1)} %bitcast.106, s32[16384]{0:T(1024)S(1)} %fusion.12), kind=kCustom, calls=%fused_computation.1.clone | custom fusion | bytes 589824 | tf_op jit(solution)/shard_map/jit(_take)/gather | solution.py:83
  124.0 11.8 %broadcast_select_fusion.1 = f32[16384,4]{1,0:T(8,128)S(1)} fusion(f32[16384,4]{1,0:T(8,128)} %gather_fusion.1, pred[16384]{0:T(1024)(128)(4,1)S(1)} %compare_and_fusion), kind=kLoop, calls=%fused_computation.5 | loop fusion | flops 65536 | bytes 540672 | tf_op jit(solution)/shard_map/jit(_take)/select_n | solution.py:83
  135.8 2.8 %fusion.15 = (f32[4,1,4096]{0,2,1:T(8,128)}, f32[4,1,4096]{0,2,1:T(8,128)S(1)}, f32[4,1,4096]{0,2,1:T(8,128)}, f32[4,1,4096]{0,2,1:T(8,128)}) fusion(f32[4,4,4096]{0,2,1:T(8,128)S(1)} %bitcast.98), kind=kLoop, calls=%fused_computation.83 | loop fusion | bytes 524288 | tf_op jit(solution)/shard_map/slice | solution.py:86
  145.9 5.1 %bitcast_multiply_fusion.3 = (f32[1,32,128]{2,1,0:T(8,128)S(1)}, f32[1,32,128]{2,1,0:T(8,128)S(1)}) fusion(f32[1,32,128]{2,1,0:T(8,128)S(1)} %get-tuple-element.34, f32[4,1,32,128]{3,2,1,0:T(8,128)S(1)} %get-tuple-element.32, f32[]{:T(128)} %bitcast.12, f32[]{:T(128)} %bitcast.11, f32[]{:T(128)} %bitcast.10, f32[]{:T(128)} %bitcast.9, f32[]{:T(128)} %bitcast.24, ...), kind=kLoop, calls=%fused_computation.65 | loop fusion | flops 65536 | bytes 114720 | tf_op jit(solution)/shard_map/mul | solution.py:73
  151.0 4.9 %bitcast_multiply_fusion.2 = (f32[1,32,128]{2,1,0:T(8,128)S(1)}, f32[1,32,128]{2,1,0:T(8,128)S(1)}) fusion(f32[1,32,128]{2,1,0:T(8,128)S(1)} %get-tuple-element.34, f32[4,1,32,128]{3,2,1,0:T(8,128)S(1)} %get-tuple-element.32, f32[]{:T(128)} %bitcast.18, f32[]{:T(128)} %bitcast.17, f32[]{:T(128)} %bitcast.16, f32[]{:T(128)} %bitcast.15, f32[]{:T(128)} %bitcast.30, ...), kind=kLoop, calls=%fused_computation.64 | loop fusion | flops 65536 | bytes 114720 | tf_op jit(solution)/shard_map/mul | solution.py:73
  156.6 10.9 %gather_fusion.2 = f32[3072,4]{1,0:T(8,128)} fusion(f32[4,4096]{0,1:T(8,128)S(1)} %copy.55, s32[3072]{0:T(1024)S(1)} %fusion.13), kind=kCustom, calls=%fused_computation.2.clone | custom fusion | bytes 110592 | tf_op jit(solution)/shard_map/jit(_take)/gather | solution.py:76
  173.3 4.4 %collective-permute-done.11 = f32[4,4,32,1]{3,2,1,0:T(8,128)S(1)} collective-permute-done((f32[4,4,32,1]{3,2,1,0:T(8,128)S(1)}, f32[4,4,32,1]{3,2,1,0:T(8,128)S(1)}, u32[]{:S(2)}, u32[]{:S(2)}) %collective-permute-start.11) | collective-permute-done | bytes 2080 | tf_op jit(solution)/shard_map/ppermute | solution.py:18
  177.7 4.1 %collective-permute-done.12 = f32[4,4,32,1]{3,2,1,0:T(8,128)S(1)} collective-permute-done((f32[4,4,32,1]{3,2,1,0:T(8,128)S(1)}, f32[4,4,32,1]{3,2,1,0:T(8,128)S(1)}, u32[]{:S(2)}, u32[]{:S(2)}) %collective-permute-start.12) | collective-permute-done | bytes 2080 | tf_op jit(solution)/shard_map/ppermute | solution.py:21
  182.0 3.5 %collective-permute-start.13 = (f32[4,4,1,130]{3,2,1,0:T(1,128)S(1)}, f32[4,4,1,130]{3,2,1,0:T(1,128)S(1)}, u32[]{:S(2)}, u32[]{:S(2)}) collective-permute-start(f32[4,4,1,130]{3,2,1,0:T(1,128)S(1)} %get-tuple-element.55), channel_id=1, source_target_pairs={{0,4},{4,8},{8,12},{1,5},{5,9},{9,13},{2,6},{6,10},{10,14},{3,7},{... | collective-permute-start | bytes 24968 | tf_op jit(solution)/shard_map/ppermute | solution.py:18
  193.9 54.8 %gather_fusion.3 = f32[16384,4]{1,0:T(8,128)} fusion(f32[4,3072]{0,1:T(8,128)S(1)} %bitcast.105, s32[16384]{0:T(1024)S(1)} %fusion.12), kind=kCustom, calls=%fused_computation.3.clone | custom fusion | bytes 589824 | tf_op jit(solution)/shard_map/jit(_take)/gather | solution.py:83
  248.6 11.8 %broadcast_select_fusion = f32[16384,4]{1,0:T(8,128)S(1)} fusion(f32[16384,4]{1,0:T(8,128)} %gather_fusion.3, pred[16384]{0:T(1024)(128)(4,1)S(1)} %compare_and_fusion), kind=kLoop, calls=%fused_computation.4 | loop fusion | flops 65536 | bytes 540672 | tf_op jit(solution)/shard_map/jit(_take)/select_n | solution.py:83
  260.4 2.8 %fusion.14 = (f32[4,1,4096]{0,2,1:T(8,128)}, f32[4,1,4096]{0,2,1:T(8,128)S(1)}, f32[4,1,4096]{0,2,1:T(8,128)}, f32[4,1,4096]{0,2,1:T(8,128)}) fusion(f32[4,4,4096]{0,2,1:T(8,128)S(1)} %bitcast.97), kind=kLoop, calls=%fused_computation.82 | loop fusion | bytes 524288 | tf_op jit(solution)/shard_map/slice | solution.py:86
  (82 shorter events, 47.9 us)
Async XLA Ops:
  30.1 4.5 %copy-start.1 = (f32[1,2,4,32,128]{4,3,2,1,0:T(8,128)S(1)}, f32[1,2,4,32,128]{4,3,2,1,0:T(8,128)}, u32[]{:S(2)}) copy-start(f32[1,2,4,32,128]{4,3,2,1,0:T(8,128)} %param.19) | copy-start | bytes 393220
  30.1 4.5 %copy-start.2 = (f32[1,4,32,128]{3,2,1,0:T(8,128)S(1)}, f32[1,4,32,128]{3,2,1,0:T(8,128)}, u32[]{:S(2)}) copy-start(f32[1,4,32,128]{3,2,1,0:T(8,128)} %param.18) | copy-start | bytes 196612
  30.1 7.6 %copy-start = (f32[1,4,4,32,128]{4,3,2,1,0:T(8,128)S(1)}, f32[1,4,4,32,128]{4,3,2,1,0:T(8,128)}, u32[]{:S(2)}) copy-start(f32[1,4,4,32,128]{4,3,2,1,0:T(8,128)} %param.17) | copy-start | bytes 786436
  30.2 8.2 %copy-start.3 = (s32[1,4,32,128]{3,2,1,0:T(8,128)S(1)}, s32[1,4,32,128]{3,2,1,0:T(8,128)}, u32[]{:S(2)}) copy-start(s32[1,4,32,128]{3,2,1,0:T(8,128)} %param.24) | copy-start | bytes 196612
  30.2 8.2 %copy-start.4 = (f32[1,4,32,128]{3,2,1,0:T(8,128)S(1)}, f32[1,4,32,128]{3,2,1,0:T(8,128)}, u32[]{:S(2)}) copy-start(f32[1,4,32,128]{3,2,1,0:T(8,128)} %param.25) | copy-start | bytes 196612
  30.4 37.0 %collective-permute-start.8 = (f32[4,1024]{1,0:T(4,128)S(1)}, f32[4,1024]{1,0:T(4,128)S(1)}, u32[]{:S(2)}, u32[]{:S(2)}) collective-permute-start(f32[4,1024]{1,0:T(4,128)S(1)} %bitcast.134), channel_id=1, source_target_pairs={{0,1},{1,2},{2,3},{3,0},{4,5},{5,6},{6,7},{7,4},{8,9},{9,10},{10,1... | collective-permute-start | bytes 49160 | tf_op jit(solution)/shard_map/ppermute | solution.py:29
  33.6 33.8 %collective-permute-start.9 = (f32[4,1024]{1,0:T(4,128)S(1)}, f32[4,1024]{1,0:T(4,128)S(1)}, u32[]{:S(2)}, u32[]{:S(2)}) collective-permute-start(f32[4,1024]{1,0:T(4,128)S(1)} %bitcast.135), channel_id=1, source_target_pairs={{0,3},{1,0},{2,1},{3,2},{4,7},{5,4},{6,5},{7,6},{8,11},{9,8},{10,9... | collective-permute-start | bytes 49160 | tf_op jit(solution)/shard_map/ppermute | solution.py:29
  34.7 8.8 %collective-permute-start = (f32[3,4,32,1]{3,2,1,0:T(8,128)S(1)}, f32[3,4,32,1]{3,2,1,0:T(8,128)S(1)}, u32[]{:S(2)}, u32[]{:S(2)}) collective-permute-start(f32[3,4,32,1]{3,2,1,0:T(8,128)S(1)} %get-tuple-element.70), channel_id=1, source_target_pairs={{0,1},{1,2},{2,3},{3,0},{4,5},{5,6},{6,7},{7,4},{8,9},{9,10},{10,1... | collective-permute-start | bytes 4616 | tf_op jit(solution)/shard_map/ppermute | solution.py:18
  35.8 12.4 %collective-permute-start.1 = (f32[3,4,32,1]{3,2,1,0:T(8,128)S(1)}, f32[3,4,32,1]{3,2,1,0:T(8,128)S(1)}, u32[]{:S(2)}, u32[]{:S(2)}) collective-permute-start(f32[3,4,32,1]{3,2,1,0:T(8,128)S(1)} %get-tuple-element.71), channel_id=1, source_target_pairs={{1,0},{2,1},{3,2},{0,3},{5,4},{6,5},{7,6},{4,7},{9,8},{10,9},{11,1... | collective-permute-start | bytes 4616 | tf_op jit(solution)/shard_map/ppermute | solution.py:21
  37.8 15.5 %collective-permute-start.4 = (f32[4,4,32,1]{3,2,1,0:T(8,128)S(1)}, f32[4,4,32,1]{3,2,1,0:T(8,128)S(1)}, u32[]{:S(2)}, u32[]{:S(2)}) collective-permute-start(f32[4,4,32,1]{3,2,1,0:T(8,128)S(1)} %get-tuple-element.68), channel_id=1, source_target_pairs={{0,1},{1,2},{2,3},{3,0},{4,5},{5,6},{6,7},{7,4},{8,9},{9,10},{10,1... | collective-permute-start | bytes 6152 | tf_op jit(solution)/shard_map/ppermute | solution.py:18
  43.5 14.2 %collective-permute-start.5 = (f32[4,4,32,1]{3,2,1,0:T(8,128)S(1)}, f32[4,4,32,1]{3,2,1,0:T(8,128)S(1)}, u32[]{:S(2)}, u32[]{:S(2)}) collective-permute-start(f32[4,4,32,1]{3,2,1,0:T(8,128)S(1)} %get-tuple-element.69), channel_id=1, source_target_pairs={{1,0},{2,1},{3,2},{0,3},{5,4},{6,5},{7,6},{4,7},{9,8},{10,9},{11,1... | collective-permute-start | bytes 6152 | tf_op jit(solution)/shard_map/ppermute | solution.py:21
  48.4 13.0 %collective-permute-start.2 = (f32[3,4,1,130]{3,2,1,0:T(1,128)S(1)}, f32[3,4,1,130]{3,2,1,0:T(1,128)S(1)}, u32[]{:S(2)}, u32[]{:S(2)}) collective-permute-start(f32[3,4,1,130]{3,2,1,0:T(1,128)S(1)} %get-tuple-element.59), channel_id=1, source_target_pairs={{0,4},{4,8},{8,12},{1,5},{5,9},{9,13},{2,6},{6,10},{10,14},{3,7},{... | collective-permute-start | bytes 18728 | tf_op jit(solution)/shard_map/ppermute | solution.py:18
  53.3 9.4 %collective-permute-start.3 = (f32[3,4,1,130]{3,2,1,0:T(1,128)S(1)}, f32[3,4,1,130]{3,2,1,0:T(1,128)S(1)}, u32[]{:S(2)}, u32[]{:S(2)}) collective-permute-start(f32[3,4,1,130]{3,2,1,0:T(1,128)S(1)} %get-tuple-element.60), channel_id=1, source_target_pairs={{4,0},{8,4},{12,8},{5,1},{9,5},{13,9},{6,2},{10,6},{14,10},{7,3},{... | collective-permute-start | bytes 18728 | tf_op jit(solution)/shard_map/ppermute | solution.py:21
  57.9 5.1 %collective-permute-start.6 = (f32[4,4,1,130]{3,2,1,0:T(1,128)S(1)}, f32[4,4,1,130]{3,2,1,0:T(1,128)S(1)}, u32[]{:S(2)}, u32[]{:S(2)}) collective-permute-start(f32[4,4,1,130]{3,2,1,0:T(1,128)S(1)} %get-tuple-element.57), channel_id=1, source_target_pairs={{0,4},{4,8},{8,12},{1,5},{5,9},{9,13},{2,6},{6,10},{10,14},{3,7},{... | collective-permute-start | bytes 24968 | tf_op jit(solution)/shard_map/ppermute | solution.py:18
  61.4 5.6 %collective-permute-start.7 = (f32[4,4,1,130]{3,2,1,0:T(1,128)S(1)}, f32[4,4,1,130]{3,2,1,0:T(1,128)S(1)}, u32[]{:S(2)}, u32[]{:S(2)}) collective-permute-start(f32[4,4,1,130]{3,2,1,0:T(1,128)S(1)} %get-tuple-element.58), channel_id=1, source_target_pairs={{4,0},{8,4},{12,8},{5,1},{9,5},{13,9},{6,2},{10,6},{14,10},{7,3},{... | collective-permute-start | bytes 24968 | tf_op jit(solution)/shard_map/ppermute | solution.py:21
  67.4 1.3 collective-permute-start.10
  167.6 10.1 %collective-permute-start.11 = (f32[4,4,32,1]{3,2,1,0:T(8,128)S(1)}, f32[4,4,32,1]{3,2,1,0:T(8,128)S(1)}, u32[]{:S(2)}, u32[]{:S(2)}) collective-permute-start(f32[4,4,32,1]{3,2,1,0:T(8,128)S(1)} %get-tuple-element.66), channel_id=1, source_target_pairs={{0,1},{1,2},{2,3},{3,0},{4,5},{5,6},{6,7},{7,4},{8,9},{9,10},{10,1... | collective-permute-start | bytes 6152 | tf_op jit(solution)/shard_map/ppermute | solution.py:18
  168.4 13.3 %collective-permute-start.12 = (f32[4,4,32,1]{3,2,1,0:T(8,128)S(1)}, f32[4,4,32,1]{3,2,1,0:T(8,128)S(1)}, u32[]{:S(2)}, u32[]{:S(2)}) collective-permute-start(f32[4,4,32,1]{3,2,1,0:T(8,128)S(1)} %get-tuple-element.67), channel_id=1, source_target_pairs={{1,0},{2,1},{3,2},{0,3},{5,4},{6,5},{7,6},{4,7},{9,8},{10,9},{11,1... | collective-permute-start | bytes 6152 | tf_op jit(solution)/shard_map/ppermute | solution.py:21
  182.0 8.6 %collective-permute-start.13 = (f32[4,4,1,130]{3,2,1,0:T(1,128)S(1)}, f32[4,4,1,130]{3,2,1,0:T(1,128)S(1)}, u32[]{:S(2)}, u32[]{:S(2)}) collective-permute-start(f32[4,4,1,130]{3,2,1,0:T(1,128)S(1)} %get-tuple-element.55), channel_id=1, source_target_pairs={{0,4},{4,8},{8,12},{1,5},{5,9},{9,13},{2,6},{6,10},{10,14},{3,7},{... | collective-permute-start | bytes 24968 | tf_op jit(solution)/shard_map/ppermute | solution.py:18
  185.5 5.6 %collective-permute-start.14 = (f32[4,4,1,130]{3,2,1,0:T(1,128)S(1)}, f32[4,4,1,130]{3,2,1,0:T(1,128)S(1)}, u32[]{:S(2)}, u32[]{:S(2)}) collective-permute-start(f32[4,4,1,130]{3,2,1,0:T(1,128)S(1)} %get-tuple-element.56), channel_id=1, source_target_pairs={{4,0},{8,4},{12,8},{5,1},{9,5},{13,9},{6,2},{10,6},{14,10},{7,3},{... | collective-permute-start | bytes 24968 | tf_op jit(solution)/shard_map/ppermute | solution.py:21
  187.1 4.7 %collective-permute-start.15 = (f32[4,1024]{1,0:T(4,128)S(1)}, f32[4,1024]{1,0:T(4,128)S(1)}, u32[]{:S(2)}, u32[]{:S(2)}) collective-permute-start(f32[4,1024]{1,0:T(4,128)S(1)} %bitcast.136), channel_id=1, source_target_pairs={{0,1},{1,2},{2,3},{3,0},{4,5},{5,6},{6,7},{7,4},{8,9},{9,10},{10,1... | collective-permute-start | bytes 49160 | tf_op jit(solution)/shard_map/ppermute | solution.py:29
  187.9 4.1 %collective-permute-start.16 = (f32[4,1024]{1,0:T(4,128)S(1)}, f32[4,1024]{1,0:T(4,128)S(1)}, u32[]{:S(2)}, u32[]{:S(2)}) collective-permute-start(f32[4,1024]{1,0:T(4,128)S(1)} %bitcast.137), channel_id=1, source_target_pairs={{0,3},{1,0},{2,1},{3,2},{4,7},{5,4},{6,5},{7,6},{8,11},{9,8},{10,9... | collective-permute-start | bytes 49160 | tf_op jit(solution)/shard_map/ppermute | solution.py:29
  192.0 1.3 collective-permute-start.17
where the time goes:
time: 274 us; the launch traced here: 271 us
  local copies, waits for them, and re-layouts  158 us (58%)
  other arithmetic  56.3 us (21%)
  starting transfers between devices  29.2 us (11%)
  waiting for transfers between devices  27.2 us (10%)
    gather x2, local copies, waits for them, and re-layouts, couple(): jnp.take(received, slot_list.reshape(-1), axis=1)  110 us
    select_n x2, other arithmetic, couple(): jnp.take(received, slot_list.reshape(-1), axis=1)  23.5 us
    mul x5, other arithmetic, couple(): fluxes.append(weight_sea * total)  22.3 us
    gather x2, local copies, waits for them, and re-layouts, couple(): jnp.take(flux, send_list.reshape(-1), axis=1)  21.8 us
    ppermute x6, waiting for transfers between devices, padded_2(): lax.ppermute(lax.slice_in_dim(block, 0, width, axis=dim), axis, backward)  15.3 us
    squeeze x8, local copies, waits for them, and re-layouts, couple(): total = total + weight_list[which][None, :] * picked_all[:, which]  14.6 us
    ppermute x6, starting transfers between devices, padded_2(): lax.ppermute(lax.slice_in_dim(block, block.shape[dim] - width, None, axis...  13 us
    ppermute x6, waiting for transfers between devices, padded_2(): lax.ppermute(lax.slice_in_dim(block, block.shape[dim] - width, None, axis...  10.7 us
  transfers between devices with their start and end apart: 18, of which 11 were waited for; matrix products, arithmetic and copies ran while one was open for 3% of the time, Pallas kernels for 0%

commit v1 on v0

v1 whole, which is shorter than its diff:
```python
import functools

import jax
import jax.numpy as jnp
from jax import lax
from jax.experimental import pallas as pl
from jax.experimental.pallas import tpu as pltpu
from jax.sharding import PartitionSpec as P

MESH = pl.DeviceIdType.MESH
STEPS = 2
ROWS = 8
LANES = 128
ALONG_LANES = lax.GatherDimensionNumbers(
    offset_dims=(),
    collapsed_slice_dims=(1,),
    start_index_map=(1,),
    operand_batching_dims=(0,),
    start_indices_batching_dims=(0,),
)


def pick_lanes(row, lanes):
    return lax.gather(
        jnp.broadcast_to(row, lanes.shape),
        lanes[..., None],
        ALONG_LANES,
        slice_sizes=(1, 1),
        mode=lax.GatherScatterMode.PROMISE_IN_BOUNDS,
    )


def kernel(
    n_lat,
    n_lon,
    adjoint,
    diffusivity,
    velocity,
    sensitivity,
    sea_mask,
    coast_distance,
    send_cells,
    recv_slots,
    regrid_weight,
    out,
    field,
    coef,
    sea,
    flux,
    cells,
    lists,
    received,
    cols_out,
    cols_east,
    cols_west,
    rows_first,
    rows_last,
    rows_north,
    rows_south,
    list_send,
    list_recv,
    halo_send,
    halo_recv,
):
    comp, lev, tlat, tlon = adjoint.shape
    terms = recv_slots.shape[0]
    blocks = send_cells.shape[1] // LANES
    planes = [(k, l) for k in range(comp) for l in range(lev)]
    sec, lat, lon = (lax.axis_index(name) for name in ("sec", "lat", "lon"))
    other = 1 - sec
    east, west = lax.rem(lon + 1, n_lon), lax.rem(lon + n_lon - 1, n_lon)
    has_south, has_north = lat > 0, lat < n_lat - 1
    sources = (west, lon, east)

    barrier = pltpu.get_barrier_semaphore()

    def greet(sec_to, lat_to, lon_to):
        pl.semaphore_signal(
            barrier, inc=1, device_id=(sec_to, lat_to, lon_to), device_id_type=MESH
        )

    for target in sources:
        greet(other, lat, target)
    greet(sec, lat, west)
    greet(sec, lat, east)
    pl.when(has_south)(lambda: greet(sec, lat - 1, lon))
    pl.when(has_north)(lambda: greet(sec, lat + 1, lon))

    def remote(src, dst, send, recv, device):
        return pltpu.make_async_remote_copy(
            src_ref=src,
            dst_ref=dst,
            send_sem=send,
            recv_sem=recv,
            device_id=device,
            device_id_type=MESH,
        )

    def list_copy(step, d):
        return remote(
            lists.at[step, d],
            received.at[step, 2 - d],
            list_send.at[step, d],
            list_recv.at[step, 2 - d],
            (other, lat, sources[d]),
        )

    def halo_copies(step):
        def one(which, src, dst, device):
            return remote(
                src.at[step],
                dst.at[step],
                halo_send.at[step, which],
                halo_recv.at[step, which],
                device,
            )

        return (
            one(0, cols_out, cols_east, (sec, lat, west)),
            one(1, cols_out, cols_west, (sec, lat, east)),
            one(2, rows_first, rows_north, (sec, lat - 1, lon)),
            one(3, rows_last, rows_south, (sec, lat + 1, lon)),
        )

    lane = lax.broadcasted_iota(jnp.int32, (tlat, tlon), 1)
    line = lax.broadcasted_iota(jnp.int32, (tlat, tlon), 0)

    distance = coast_distance[...].astype(jnp.float32)
    sea[...] = sea_mask[...].astype(jnp.float32) * ((distance + 1.0) / (distance + 9.0))
    for d in range(3):
        for j in range(blocks):
            cells[d, j : j + 1, :] = send_cells[d : d + 1, j * LANES : (j + 1) * LANES]
    for l in range(lev):
        spread = diffusivity[l]
        half_x, half_y = 0.5 * velocity[0, l], 0.5 * velocity[1, l]
        coef[0, l] = spread + half_x
        coef[1, l] = spread - half_x
        coef[2, l] = spread + half_y
        coef[3, l] = spread - half_y
        coef[4, l] = 1.0 - 4.0 * spread

    def send_lists(step, src):
        for k in range(comp):
            total = sensitivity[k, 0] * src[0, 0]
            for j in range(1, comp):
                total = total + sensitivity[k, j] * src[j, 0]
            flux[k] = sea[...] * total
        for d in (0, 2, 1):
            index = cells[d]
            lanes, row = index & (LANES - 1), index >> 7
            found = [jnp.zeros((blocks, LANES), jnp.float32)] * comp
            for r in range(tlat):
                here = row == r
                for k in range(comp):
                    found[k] = jnp.where(
                        here, pick_lanes(flux[k, r : r + 1, :], lanes), found[k]
                    )
            for k in range(comp):
                lists[step, d, k] = found[k]
            if step == 0 and d == 0:
                pl.semaphore_wait(
                    barrier, 5 + has_south.astype(jnp.int32) + has_north.astype(jnp.int32)
                )
            list_copy(step, d).start()

    def inner(step, src, dst):
        packed = jnp.zeros((tlat, tlon), jnp.float32)
        for p, (k, l) in enumerate(planes):
            value = src[k, l]
            to_west = pltpu.roll(coef[0, l] * value, tlon - 1, 1)
            to_east = pltpu.roll(coef[1, l] * value, 1, 1)
            rim = jnp.where(lane == tlon - 1, to_west, to_east)
            packed = jnp.where(lane >> 1 == p, pltpu.roll(rim, 2 * p + 1, 1), packed)
            to_south, to_north = coef[2, l] * value, coef[3, l] * value
            rows_first[step, p : p + 1, :] = to_south[0:1]
            rows_last[step, p : p + 1, :] = to_north[tlat - 1 : tlat]
            dst[k, l] = (
                coef[4, l] * value
                + jnp.where(lane == tlon - 1, 0.0, to_west)
                + jnp.where(lane == 0, 0.0, to_east)
                + jnp.where(line == tlat - 1, 0.0, pltpu.roll(to_south, tlat - 1, 0))
                + jnp.where(line == 0, 0.0, pltpu.roll(to_north, 1, 0))
            )
        cols_out[step] = packed
        copies = halo_copies(step)
        copies[0].start()
        copies[1].start()
        pl.when(has_south)(copies[2].start)
        pl.when(has_north)(copies[3].start)

    def rims(step, dst):
        copies = halo_copies(step)
        copies[0].wait_recv()
        copies[1].wait_recv()
        both = jnp.where(lane & 1 == 0, cols_east[step], cols_west[step])
        edge = (lane == 0) | (lane == tlon - 1)
        for p, (k, l) in enumerate(planes):
            turned = pltpu.roll(both, tlon - 1 - 2 * p, 1)
            dst[k, l] = dst[k, l] + jnp.where(edge, turned, 0.0)

        @pl.when(has_north)
        def _():
            copies[2].wait_recv()
            for p, (k, l) in enumerate(planes):
                dst[k, l, tlat - 1 : tlat, :] += rows_north[step, p : p + 1, :]

        @pl.when(has_south)
        def _():
            copies[3].wait_recv()
            for p, (k, l) in enumerate(planes):
                dst[k, l, 0:1, :] += rows_south[step, p : p + 1, :]

    def regrid(step, dst):
        for d in range(3):
            list_copy(step, d).wait_recv()

        def some(g, carry):
            where = pl.ds(pl.multiple_of(g * ROWS, ROWS), ROWS)
            index = [recv_slots[t, where, :] for t in range(terms)]
            lanes = [i & (LANES - 1) for i in index]
            row = [i >> 7 for i in index]
            found = [[jnp.zeros((ROWS, tlon), jnp.float32)] * comp for t in range(terms)]
            for r in range(3 * blocks):
                here = [i == r for i in row]
                for k in range(comp):
                    source = received[step, r // blocks, k, r % blocks : r % blocks + 1, :]
                    for t in range(terms):
                        found[t][k] = jnp.where(
                            here[t], pick_lanes(source, lanes[t]), found[t][k]
                        )
            for k in range(comp):
                total = dst[k, 0, where, :]
                for t in range(terms):
                    total = total + regrid_weight[t, where, :] * found[t][k]
                dst[k, 0, where, :] = total
            return carry

        lax.fori_loop(0, tlat // ROWS, some, 0)

    for step, (src, dst) in enumerate(((adjoint, field), (field, out))):
        send_lists(step, src)
        inner(step, src, dst)
        rims(step, dst)
        regrid(step, dst)

    for step in range(STEPS):
        for d in range(3):
            list_copy(step, d).wait_send()
        copies = halo_copies(step)
        copies[0].wait_send()
        copies[1].wait_send()
        pl.when(has_south)(copies[2].wait_send)
        pl.when(has_north)(copies[3].wait_send)


def on_device(n_lat, n_lon, *arrays):
    arrays = [array[0] for array in arrays]
    arrays[6] = arrays[6][0]
    adjoint, send_cells = arrays[0], arrays[6]
    comp, lev, tlat, tlon = adjoint.shape
    blocks = send_cells.shape[1] // LANES
    planes = comp * lev
    vmem = pl.BlockSpec(memory_space=pltpu.VMEM)
    specs = [vmem] * len(arrays)
    specs[3] = pl.BlockSpec(memory_space=pltpu.SMEM)
    f32 = jnp.float32
    result = pl.pallas_call(
        functools.partial(kernel, n_lat, n_lon),
        out_shape=jax.ShapeDtypeStruct(adjoint.shape, f32),
        in_specs=specs,
        out_specs=vmem,
        scratch_shapes=[
            pltpu.VMEM(adjoint.shape, f32),
            pltpu.VMEM((5, lev, tlat, tlon), f32),
            pltpu.VMEM((tlat, tlon), f32),
            pltpu.VMEM((comp, tlat, tlon), f32),
            pltpu.VMEM((3, blocks, LANES), jnp.int32),
            pltpu.VMEM((STEPS, 3, comp, blocks, LANES), f32),
            pltpu.VMEM((STEPS, 3, comp, blocks, LANES), f32),
            pltpu.VMEM((STEPS, tlat, tlon), f32),
            pltpu.VMEM((STEPS, tlat, tlon), f32),
            pltpu.VMEM((STEPS, tlat, tlon), f32),
            pltpu.VMEM((STEPS, planes, tlon), f32),
            pltpu.VMEM((STEPS, planes, tlon), f32),
            pltpu.VMEM((STEPS, planes, tlon), f32),
            pltpu.VMEM((STEPS, planes, tlon), f32),
            pltpu.SemaphoreType.DMA((STEPS, 3)),
            pltpu.SemaphoreType.DMA((STEPS, 3)),
            pltpu.SemaphoreType.DMA((STEPS, 4)),
            pltpu.SemaphoreType.DMA((STEPS, 4)),
        ],
        compiler_params=pltpu.CompilerParams(
            collective_id=0, has_side_effects=True, vmem_limit_bytes=16 * 1024 * 1024
        ),
        cost_estimate=pl.CostEstimate(
            flops=4_000_000, bytes_accessed=900_000, transcendentals=0
        ),
    )(*arrays)
    return result[None]


def solution(mesh):
    placed = (
        P("sec", None, None, "lat", "lon"),
        P("sec", None, "lat", "lon"),
        P("sec", None, None, "lat", "lon"),
        P("sec", None, None),
        P("sec", "lat", "lon"),
        P("sec", "lat", "lon"),
        P("sec", "lat", "lon", None),
        P("sec", None, "lat", "lon"),
        P("sec", None, "lat", "lon"),
    )
    return jax.shard_map(
        functools.partial(on_device, mesh.shape["lat"], mesh.shape["lon"]),
        mesh=mesh,
        in_specs=placed,
        out_specs=P("sec", None, None, "lat", "lon"),
        check_vma=False,
    )
```

time: 274 us -> 29.6 us (0.11)
  local copies, waits for them, and re-layouts: 158 us -> 5.83 us
  other arithmetic: 56.3 us -> 0 us
  starting transfers between devices: 29.2 us -> 0 us
  waiting for transfers between devices: 27.2 us -> 0 us
  Pallas kernels: 0 us -> 23.3 us
    gather x4 -> x0, local copies, waits for them, and re-layouts: 131 us -> none  [the longest x2 110 us: couple(): jnp.take(received, slot_list.reshape(-1), axis=1)]
    ppermute x18 -> x0, starting transfers between devices: 29.2 us -> none  [the longest x6 13 us: padded_2(): lax.ppermute(lax.slice_in_dim(block, block.shape[dim] - width, None, axis...]
    select_n x4 -> x0, other arithmetic: 28.9 us -> none  [the longest x2 23.5 us: couple(): jnp.take(received, slot_list.reshape(-1), axis=1)]
    ppermute x18 -> x0, waiting for transfers between devices: 27.2 us -> none  [the longest x6 15.3 us: padded_2(): lax.ppermute(lax.slice_in_dim(block, 0, width, axis=dim), axis, backward)]
    pallas_call x0 -> x1, Pallas kernels: none -> 23.3 us  [on_device(): pl.pallas_call(functools.partial(kernel, n_lat, n_lon), out_shape=jax.Sha...]
    mul x7 -> x0, other arithmetic: 23.1 us -> none  [the longest x5 22.3 us: couple(): fluxes.append(weight_sea * total)]
    squeeze x8 -> x0, local copies, waits for them, and re-layouts: 14.6 us -> none  [couple(): total = total + weight_list[which][None, :] * picked_all[:, which]]
    slice x7 -> x0, local copies, waits for them, and re-layouts: 7.97 us -> none  [the longest x2 5.53 us: couple(): total = total + weight_list[which][None, :] * picked_all[:, which]]
  transfers between devices with their start and end apart: 18 -> 0, of which waited for: 11 -> 0; matrix products, arithmetic and copies ran while one was open for 3% -> 0% of each run, Pallas kernels for 0% -> 0%
where the time goes in v1:
time: 29.6 us; the launch traced here: 29.2 us
  Pallas kernels  23.3 us (79%)
  local copies, waits for them, and re-layouts  5.83 us (20%)
    pallas_call x1, Pallas kernels, on_device(): pl.pallas_call(functools.partial(kernel, n_lat, n_lon), out_shape=jax.Sha...  23.3 us
    unnamed x18, local copies, waits for them, and re-layouts  5.83 us

profile of v1, /device:TPU:0, one launch (start us, length us, event | category | flops | bytes accessed | tf_op | source)
XLA Modules:
  0.0 29.2 jit_solution(10325584557965109253)
XLA Ops:
  0.0 0.0 copy-start.7
  0.0 0.0 copy-start.6
  0.0 0.0 copy-start.5
  0.0 0.7 %copy.12 = s32[1,1,3,1024]{3,2,1,0:T(4,128)S(1)} copy(s32[1,1,3,1024]{3,1,2,0:T(1,128)} %param.15) | data formatting | bytes 24576
  0.7 0.0 copy-done.7
  0.8 0.0 copy-done.6
  0.8 0.0 copy-done.5
  0.8 0.0 copy-start
  0.8 0.9 %copy-done = f32[1,4,4,32,128]{4,3,2,1,0:T(8,128)S(1)} copy-done((f32[1,4,4,32,128]{4,3,2,1,0:T(8,128)S(1)}, f32[1,4,4,32,128]{4,3,2,1,0:T(8,128)}, u32[]{:S(2)}) %copy-start) | copy-done | bytes 262168
  1.7 0.0 copy-start.1
  1.7 0.9 %copy-done.1 = f32[1,2,4,32,128]{4,3,2,1,0:T(8,128)S(1)} copy-done((f32[1,2,4,32,128]{4,3,2,1,0:T(8,128)S(1)}, f32[1,2,4,32,128]{4,3,2,1,0:T(8,128)}, u32[]{:S(2)}) %copy-start.1) | copy-done | bytes 131096
  2.6 0.0 copy-start.2
  2.6 0.8 %copy-done.2 = f32[1,4,32,128]{3,2,1,0:T(8,128)S(1)} copy-done((f32[1,4,32,128]{3,2,1,0:T(8,128)S(1)}, f32[1,4,32,128]{3,2,1,0:T(8,128)}, u32[]{:S(2)}) %copy-start.2) | copy-done | bytes 65560
  3.5 0.0 copy-start.3
  3.5 0.8 %copy-done.3 = s32[1,4,32,128]{3,2,1,0:T(8,128)S(1)} copy-done((s32[1,4,32,128]{3,2,1,0:T(8,128)S(1)}, s32[1,4,32,128]{3,2,1,0:T(8,128)}, u32[]{:S(2)}) %copy-start.3) | copy-done | bytes 65560
  4.3 0.0 copy-start.4
  4.3 0.8 %copy-done.4 = f32[1,4,32,128]{3,2,1,0:T(8,128)S(1)} copy-done((f32[1,4,32,128]{3,2,1,0:T(8,128)S(1)}, f32[1,4,32,128]{3,2,1,0:T(8,128)}, u32[]{:S(2)}) %copy-start.4) | copy-done | bytes 65560
  5.1 23.3 %shard_map.91 = f32[4,4,32,128]{3,2,1,0:T(8,128)S(1)} custom-call(f32[4,4,32,128]{3,2,1,0:T(8,128)S(1)} %bitcast.13, f32[4,32,128]{2,1,0:T(8,128)S(1)} %bitcast.16, f32[2,4,32,128]{3,2,1,0:T(8,128)S(1)} %bitcast.14, f32[4,4]{1,0:T(4,128)S(1)} %bitcast.21, s32[32,128]{1,0:T(8,128)S(1)} %bitcast.19, s32[32,128]{1,0:T(8,128)S(1)} %bitcast.20, ...), custom_call_target="tpu_custom_call" | custom-call | flops 4000000 | bytes 900000 | tf_op jit(solution)/shard_map/pallas_call | solution.py:267
  28.5 0.7 %copy.14 = f32[1,4,4,32,128]{4,3,2,1,0:T(8,128)} copy(f32[1,4,4,32,128]{4,3,2,1,0:T(8,128)S(1)} %bitcast.12) | data formatting | bytes 524288
Async XLA Ops:
  0.0 0.8 %copy-start.7 = (f32[1,4,4]{2,1,0:T(4,128)S(1)}, f32[1,4,4]{2,1,0:T(4,128)}, u32[]{:S(2)}) copy-start(f32[1,4,4]{2,1,0:T(4,128)} %param.12) | copy-start | bytes 196
  0.0 0.8 %copy-start.6 = (s32[1,32,128]{2,1,0:T(8,128)S(1)}, s32[1,32,128]{2,1,0:T(8,128)}, u32[]{:S(2)}) copy-start(s32[1,32,128]{2,1,0:T(8,128)} %param.14) | copy-start | bytes 49156
  0.0 0.8 %copy-start.5 = (s32[1,32,128]{2,1,0:T(8,128)S(1)}, s32[1,32,128]{2,1,0:T(8,128)}, u32[]{:S(2)}) copy-start(s32[1,32,128]{2,1,0:T(8,128)} %param.13) | copy-start | bytes 49156
  0.8 1.0 %copy-start = (f32[1,4,4,32,128]{4,3,2,1,0:T(8,128)S(1)}, f32[1,4,4,32,128]{4,3,2,1,0:T(8,128)}, u32[]{:S(2)}) copy-start(f32[1,4,4,32,128]{4,3,2,1,0:T(8,128)} %param.9) | copy-start | bytes 786436
  1.7 0.9 %copy-start.1 = (f32[1,2,4,32,128]{4,3,2,1,0:T(8,128)S(1)}, f32[1,2,4,32,128]{4,3,2,1,0:T(8,128)}, u32[]{:S(2)}) copy-start(f32[1,2,4,32,128]{4,3,2,1,0:T(8,128)} %param.11) | copy-start | bytes 393220
  2.6 0.8 %copy-start.2 = (f32[1,4,32,128]{3,2,1,0:T(8,128)S(1)}, f32[1,4,32,128]{3,2,1,0:T(8,128)}, u32[]{:S(2)}) copy-start(f32[1,4,32,128]{3,2,1,0:T(8,128)} %param.10) | copy-start | bytes 196612
  3.5 0.8 %copy-start.3 = (s32[1,4,32,128]{3,2,1,0:T(8,128)S(1)}, s32[1,4,32,128]{3,2,1,0:T(8,128)}, u32[]{:S(2)}) copy-start(s32[1,4,32,128]{3,2,1,0:T(8,128)} %param.16) | copy-start | bytes 196612
  4.3 0.8 %copy-start.4 = (f32[1,4,32,128]{3,2,1,0:T(8,128)S(1)}, f32[1,4,32,128]{3,2,1,0:T(8,128)}, u32[]{:S(2)}) copy-start(f32[1,4,32,128]{3,2,1,0:T(8,128)} %param.17) | copy-start | bytes 196612

commit v2 on v1

--- a/solution.py
+++ b/solution.py
@@ -33,21 +33,14 @@
 def kernel(
     n_lat,
     n_lon,
-    adjoint,
-    diffusivity,
-    velocity,
-    sensitivity,
-    sea_mask,
-    coast_distance,
-    send_cells,
-    recv_slots,
-    regrid_weight,
-    out,
+    *refs,
+):
+    inputs, out = refs[:9], refs[9]
+    held, (
     field,
     coef,
     sea,
     flux,
-    cells,
     lists,
     received,
     cols_out,
@@ -61,10 +54,28 @@
     list_recv,
     halo_send,
     halo_recv,
-):
+    load_sem,
+    ) = refs[10:19], refs[19:]
+    (
+        adjoint,
+        diffusivity,
+        velocity,
+        sensitivity,
+        sea_mask,
+        coast_distance,
+        cells,
+        recv_slots,
+        regrid_weight,
+    ) = held
+    loads = [
+        pltpu.make_async_copy(inputs[i], held[i], load_sem.at[i]) for i in range(9)
+    ]
+    for i in (0, 6, 4, 5, 3, 1, 2, 7, 8):
+        loads[i].start()
+
     comp, lev, tlat, tlon = adjoint.shape
     terms = recv_slots.shape[0]
-    blocks = send_cells.shape[1] // LANES
+    blocks = cells.shape[1]
     planes = [(k, l) for k in range(comp) for l in range(lev)]
     sec, lat, lon = (lax.axis_index(name) for name in ("sec", "lat", "lon"))
     other = 1 - sec
@@ -125,19 +136,22 @@
     lane = lax.broadcasted_iota(jnp.int32, (tlat, tlon), 1)
     line = lax.broadcasted_iota(jnp.int32, (tlat, tlon), 0)
 
+    for i in (4, 5, 3, 0, 6):
+        loads[i].wait()
     distance = coast_distance[...].astype(jnp.float32)
     sea[...] = sea_mask[...].astype(jnp.float32) * ((distance + 1.0) / (distance + 9.0))
-    for d in range(3):
-        for j in range(blocks):
-            cells[d, j : j + 1, :] = send_cells[d : d + 1, j * LANES : (j + 1) * LANES]
-    for l in range(lev):
-        spread = diffusivity[l]
-        half_x, half_y = 0.5 * velocity[0, l], 0.5 * velocity[1, l]
-        coef[0, l] = spread + half_x
-        coef[1, l] = spread - half_x
-        coef[2, l] = spread + half_y
-        coef[3, l] = spread - half_y
-        coef[4, l] = 1.0 - 4.0 * spread
+
+    def coefficients():
+        loads[1].wait()
+        loads[2].wait()
+        for l in range(lev):
+            spread = diffusivity[l]
+            half_x, half_y = 0.5 * velocity[0, l], 0.5 * velocity[1, l]
+            coef[0, l] = spread + half_x
+            coef[1, l] = spread - half_x
+            coef[2, l] = spread + half_y
+            coef[3, l] = spread - half_y
+            coef[4, l] = 1.0 - 4.0 * spread
 
     def send_lists(step, src):
         for k in range(comp):
@@ -220,14 +234,12 @@
             lanes = [i & (LANES - 1) for i in index]
             row = [i >> 7 for i in index]
             found = [[jnp.zeros((ROWS, tlon), jnp.float32)] * comp for t in range(terms)]
-            for r in range(3 * blocks):
-                here = [i == r for i in row]
-                for k in range(comp):
-                    source = received[step, r // blocks, k, r % blocks : r % blocks + 1, :]
-                    for t in range(terms):
-                        found[t][k] = jnp.where(
-                            here[t], pick_lanes(source, lanes[t]), found[t][k]
-                        )
+            for t in range(terms):
+                for r in range(3 * blocks):
+                    here = row[t] == r
+                    for k in range(comp):
+                        source = received[step, r // blocks, k, r % blocks : r % blocks + 1, :]
+                        found[t][k] = jnp.where(here, pick_lanes(source, lanes[t]), found[t][k])
             for k in range(comp):
                 total = dst[k, 0, where, :]
                 for t in range(terms):
@@ -239,8 +251,13 @@
 
     for step, (src, dst) in enumerate(((adjoint, field), (field, out))):
         send_lists(step, src)
+        if step == 0:
+            coefficients()
         inner(step, src, dst)
         rims(step, dst)
+        if step == 0:
+            loads[7].wait()
+            loads[8].wait()
         regrid(step, dst)
 
     for step in range(STEPS):
@@ -255,14 +272,14 @@
 
 def on_device(n_lat, n_lon, *arrays):
     arrays = [array[0] for array in arrays]
-    arrays[6] = arrays[6][0]
-    adjoint, send_cells = arrays[0], arrays[6]
+    blocks = arrays[6].shape[2] // LANES
+    arrays[6] = arrays[6].reshape(3, blocks, LANES)
+    adjoint = arrays[0]
     comp, lev, tlat, tlon = adjoint.shape
-    blocks = send_cells.shape[1] // LANES
     planes = comp * lev
     vmem = pl.BlockSpec(memory_space=pltpu.VMEM)
-    specs = [vmem] * len(arrays)
-    specs[3] = pl.BlockSpec(memory_space=pltpu.SMEM)
+    specs = [pl.BlockSpec(memory_space=pltpu.HBM)] * len(arrays)
+    spaces = [pltpu.SMEM if i == 3 else pltpu.VMEM for i in range(len(arrays))]
     f32 = jnp.float32
     result = pl.pallas_call(
         functools.partial(kernel, n_lat, n_lon),
@@ -270,11 +287,11 @@
         in_specs=specs,
         out_specs=vmem,
         scratch_shapes=[
+            *(space(array.shape, array.dtype) for space, array in zip(spaces, arrays)),
             pltpu.VMEM(adjoint.shape, f32),
             pltpu.VMEM((5, lev, tlat, tlon), f32),
             pltpu.VMEM((tlat, tlon), f32),
             pltpu.VMEM((comp, tlat, tlon), f32),
-            pltpu.VMEM((3, blocks, LANES), jnp.int32),
             pltpu.VMEM((STEPS, 3, comp, blocks, LANES), f32),
             pltpu.VMEM((STEPS, 3, comp, blocks, LANES), f32),
             pltpu.VMEM((STEPS, tlat, tlon), f32),
@@ -288,9 +305,10 @@
             pltpu.SemaphoreType.DMA((STEPS, 3)),
             pltpu.SemaphoreType.DMA((STEPS, 4)),
             pltpu.SemaphoreType.DMA((STEPS, 4)),
+            pltpu.SemaphoreType.DMA((len(arrays),)),
         ],
         compiler_params=pltpu.CompilerParams(
-            collective_id=0, has_side_effects=True, vmem_limit_bytes=16 * 1024 * 1024
+            collective_id=0, has_side_effects=True, vmem_limit_bytes=60 * 1024 * 1024
         ),
         cost_estimate=pl.CostEstimate(
             flops=4_000_000, bytes_accessed=900_000, transcendentals=0

time: 29.6 us -> 19.9 us (0.67)
  Pallas kernels: 23.3 us -> 18.1 us
  local copies, waits for them, and re-layouts: 5.83 us -> 1.67 us
    pallas_call x1, Pallas kernels: 23.3 us -> 18.1 us  [on_device(): pl.pallas_call(functools.partial(kernel, n_lat, n_lon), out_shape=jax.Sha...]
    unnamed x18 -> x1, local copies, waits for them, and re-layouts: 5.83 us -> 1.67 us
where the time goes in v2:
time: 19.9 us; the launch traced here: 19.8 us
  Pallas kernels  18.1 us (91%)
  local copies, waits for them, and re-layouts  1.67 us (8%)
    pallas_call x1, Pallas kernels, on_device(): pl.pallas_call(functools.partial(kernel, n_lat, n_lon), out_shape=jax.Sha...  18.1 us
    unnamed x1, local copies, waits for them, and re-layouts  1.67 us

profile of v2, /device:TPU:0, one launch (start us, length us, event | category | flops | bytes accessed | tf_op | source)
XLA Modules:
  0.0 19.8 jit_solution(1308486481708581623)
XLA Ops:
  0.0 18.1 %shard_map.91 = f32[4,4,32,128]{3,2,1,0:T(8,128)} custom-call(f32[4,4,32,128]{3,2,1,0:T(8,128)} %bitcast.11, f32[4,32,128]{2,1,0:T(8,128)} %bitcast.13, f32[2,4,32,128]{3,2,1,0:T(8,128)} %bitcast.12, f32[4,4]{1,0:T(4,128)} %bitcast.19, s32[32,128]{1,0:T(8,128)} %bitcast.16, s32[32,128]{1,0:T(8,128)} %bitcast.17, s32[3,8,128]{2,1,0:T(8,128)} %bitcast.18, ...), custom_call_target="tpu_custom_call" | custom-call | flops 4000000 | bytes 900000 | tf_op jit(solution)/shard_map/pallas_call | solution.py:284
  18.1 1.7 %copy.11 = f32[1,4,4,32,128]{4,3,2,1,0:T(8,128)} copy(f32[1,4,4,32,128]{4,3,2,1,0:T(8,128)} %bitcast.10) | data formatting | bytes 524288

commit v3 on v2

--- a/solution.py
+++ b/solution.py
@@ -247,7 +247,7 @@
                 dst[k, 0, where, :] = total
             return carry
 
-        lax.fori_loop(0, tlat // ROWS, some, 0)
+        lax.fori_loop(0, tlat // ROWS, some, 0, unroll=True)
 
     for step, (src, dst) in enumerate(((adjoint, field), (field, out))):
         send_lists(step, src)
@@ -281,6 +281,7 @@
     specs = [pl.BlockSpec(memory_space=pltpu.HBM)] * len(arrays)
     spaces = [pltpu.SMEM if i == 3 else pltpu.VMEM for i in range(len(arrays))]
     f32 = jnp.float32
+    arrays = [pltpu.with_memory_space_constraint(a, pltpu.HBM) for a in arrays]
     result = pl.pallas_call(
         functools.partial(kernel, n_lat, n_lon),
         out_shape=jax.ShapeDtypeStruct(adjoint.shape, f32),
@@ -308,7 +309,7 @@
             pltpu.SemaphoreType.DMA((len(arrays),)),
         ],
         compiler_params=pltpu.CompilerParams(
-            collective_id=0, has_side_effects=True, vmem_limit_bytes=60 * 1024 * 1024
+            collective_id=0, has_side_effects=True, vmem_limit_bytes=16 * 1024 * 1024
         ),
         cost_estimate=pl.CostEstimate(
             flops=4_000_000, bytes_accessed=900_000, transcendentals=0

time: 19.9 us -> 17.8 us (0.89)
  Pallas kernels: 18.1 us -> 17 us
  local copies, waits for them, and re-layouts: 1.67 us -> 0.71 us
    pallas_call x1, Pallas kernels: 18.1 us -> 17 us  [on_device(): pl.pallas_call(functools.partial(kernel, n_lat, n_lon), out_shape=jax.Sha...]
    unnamed x1, local copies, waits for them, and re-layouts: 1.67 us -> 0.71 us
where the time goes in v3:
time: 17.8 us; the launch traced here: 17.7 us
  Pallas kernels  17 us (96%)
  local copies, waits for them, and re-layouts  0.71 us (4%)
    pallas_call x1, Pallas kernels, on_device(): pl.pallas_call(functools.partial(kernel, n_lat, n_lon), out_shape=jax.Sha...  17 us
    unnamed x1, local copies, waits for them, and re-layouts  0.71 us

profile of v3, /device:TPU:0, one launch (start us, length us, event | category | flops | bytes accessed | tf_op | source)
XLA Modules:
  0.0 17.7 jit_solution(13071107724911152782)
XLA Ops:
  0.0 17.0 %shard_map.91 = f32[4,4,32,128]{3,2,1,0:T(8,128)S(1)} custom-call(f32[4,4,32,128]{3,2,1,0:T(8,128)} %bitcast.11, f32[4,32,128]{2,1,0:T(8,128)} %bitcast.13, f32[2,4,32,128]{3,2,1,0:T(8,128)} %bitcast.12, f32[4,4]{1,0:T(4,128)} %bitcast.19, s32[32,128]{1,0:T(8,128)} %bitcast.16, s32[32,128]{1,0:T(8,128)} %bitcast.17, s32[3,8,128]{2,1,0:T(8,128)} %bitcast.18, ...), custom_call_target="tpu_custom_call" | custom-call | flops 4000000 | bytes 900000 | tf_op jit(solution)/shard_map/pallas_call | solution.py:285
  17.0 0.7 %copy.11 = f32[1,4,4,32,128]{4,3,2,1,0:T(8,128)} copy(f32[1,4,4,32,128]{4,3,2,1,0:T(8,128)S(1)} %bitcast.10) | data formatting | bytes 524288

commit v4 on v3

--- a/solution.py
+++ b/solution.py
@@ -41,6 +41,7 @@
     coef,
     sea,
     flux,
+    wide,
     lists,
     received,
     cols_out,
@@ -224,41 +225,42 @@
             for p, (k, l) in enumerate(planes):
                 dst[k, l, 0:1, :] += rows_south[step, p : p + 1, :]
 
-    def regrid(step, dst):
-        for d in range(3):
-            list_copy(step, d).wait_recv()
-
-        def some(g, carry):
-            where = pl.ds(pl.multiple_of(g * ROWS, ROWS), ROWS)
-            index = [recv_slots[t, where, :] for t in range(terms)]
-            lanes = [i & (LANES - 1) for i in index]
-            row = [i >> 7 for i in index]
-            found = [[jnp.zeros((ROWS, tlon), jnp.float32)] * comp for t in range(terms)]
+    def regrid(step, dst, e):
+        list_copy(step, 2 - e).wait_recv()
+        for k in range(comp):
+            for j in range(blocks):
+                wide[k, j] = jnp.broadcast_to(
+                    received[step, e, k, j : j + 1, :], (ROWS, LANES)
+                )
+        for g in range(tlat // ROWS):
+            where = slice(g * ROWS, (g + 1) * ROWS)
+            total = [dst[k, 0, where, :] for k in range(comp)]
             for t in range(terms):
-                for r in range(3 * blocks):
-                    here = row[t] == r
+                index = recv_slots[t, where, :]
+                weight = regrid_weight[t, where, :]
+                lanes, row = index & (LANES - 1), index >> 7
+                found = [jnp.zeros((ROWS, tlon), jnp.float32)] * comp
+                for j in range(blocks):
+                    here = row == e * blocks + j
                     for k in range(comp):
-                        source = received[step, r // blocks, k, r % blocks : r % blocks + 1, :]
-                        found[t][k] = jnp.where(here, pick_lanes(source, lanes[t]), found[t][k])
+                        found[k] = jnp.where(here, pick_lanes(wide[k, j], lanes), found[k])
+                for k in range(comp):
+                    total[k] = total[k] + weight * found[k]
             for k in range(comp):
-                total = dst[k, 0, where, :]
-                for t in range(terms):
-                    total = total + regrid_weight[t, where, :] * found[t][k]
-                dst[k, 0, where, :] = total
-            return carry
-
-        lax.fori_loop(0, tlat // ROWS, some, 0, unroll=True)
+                dst[k, 0, where, :] = total[k]
 
     for step, (src, dst) in enumerate(((adjoint, field), (field, out))):
         send_lists(step, src)
         if step == 0:
             coefficients()
         inner(step, src, dst)
-        rims(step, dst)
         if step == 0:
             loads[7].wait()
             loads[8].wait()
-        regrid(step, dst)
+        regrid(step, dst, 1)
+        rims(step, dst)
+        regrid(step, dst, 0)
+        regrid(step, dst, 2)
 
     for step in range(STEPS):
         for d in range(3):
@@ -293,6 +295,7 @@
             pltpu.VMEM((5, lev, tlat, tlon), f32),
             pltpu.VMEM((tlat, tlon), f32),
             pltpu.VMEM((comp, tlat, tlon), f32),
+            pltpu.VMEM((comp, blocks, ROWS, LANES), f32),
             pltpu.VMEM((STEPS, 3, comp, blocks, LANES), f32),
             pltpu.VMEM((STEPS, 3, comp, blocks, LANES), f32),
             pltpu.VMEM((STEPS, tlat, tlon), f32),

time: 17.8 us -> 16.9 us (0.949)
  Pallas kernels: 17 us -> 16 us
    pallas_call x1, Pallas kernels: 17 us -> 16 us  [on_device(): pl.pallas_call(functools.partial(kernel, n_lat, n_lon), out_shape=jax.Sha...]
where the time goes in v4:
time: 16.9 us; the launch traced here: 16.7 us
  Pallas kernels  16 us (95%)
  local copies, waits for them, and re-layouts  0.71 us (4%)
    pallas_call x1, Pallas kernels, on_device(): pl.pallas_call(functools.partial(kernel, n_lat, n_lon), out_shape=jax.Sha...  16 us
    unnamed x1, local copies, waits for them, and re-layouts  0.71 us

profile of v4, /device:TPU:0, one launch (start us, length us, event | category | flops | bytes accessed | tf_op | source)
XLA Modules:
  0.0 16.7 jit_solution(4128422741350977840)
XLA Ops:
  0.0 16.0 %shard_map.91 = f32[4,4,32,128]{3,2,1,0:T(8,128)S(1)} custom-call(f32[4,4,32,128]{3,2,1,0:T(8,128)} %bitcast.11, f32[4,32,128]{2,1,0:T(8,128)} %bitcast.13, f32[2,4,32,128]{3,2,1,0:T(8,128)} %bitcast.12, f32[4,4]{1,0:T(4,128)} %bitcast.19, s32[32,128]{1,0:T(8,128)} %bitcast.16, s32[32,128]{1,0:T(8,128)} %bitcast.17, s32[3,8,128]{2,1,0:T(8,128)} %bitcast.18, ...), custom_call_target="tpu_custom_call" | custom-call | flops 4000000 | bytes 900000 | tf_op jit(solution)/shard_map/pallas_call | solution.py:287
  16.0 0.7 %copy.11 = f32[1,4,4,32,128]{4,3,2,1,0:T(8,128)} copy(f32[1,4,4,32,128]{4,3,2,1,0:T(8,128)S(1)} %bitcast.10) | data formatting | bytes 524288

commit v5 on v4

--- a/solution.py
+++ b/solution.py
@@ -203,26 +203,30 @@
         pl.when(has_south)(copies[2].start)
         pl.when(has_north)(copies[3].start)
 
-    def rims(step, dst):
+    def rims(step, dst, levels, arrive):
         copies = halo_copies(step)
-        copies[0].wait_recv()
-        copies[1].wait_recv()
+        if arrive:
+            copies[0].wait_recv()
+            copies[1].wait_recv()
         both = jnp.where(lane & 1 == 0, cols_east[step], cols_west[step])
         edge = (lane == 0) | (lane == tlon - 1)
-        for p, (k, l) in enumerate(planes):
+        chosen = [(p, k, l) for p, (k, l) in enumerate(planes) if l in levels]
+        for p, k, l in chosen:
             turned = pltpu.roll(both, tlon - 1 - 2 * p, 1)
             dst[k, l] = dst[k, l] + jnp.where(edge, turned, 0.0)
 
         @pl.when(has_north)
         def _():
-            copies[2].wait_recv()
-            for p, (k, l) in enumerate(planes):
+            if arrive:
+                copies[2].wait_recv()
+            for p, k, l in chosen:
                 dst[k, l, tlat - 1 : tlat, :] += rows_north[step, p : p + 1, :]
 
         @pl.when(has_south)
         def _():
-            copies[3].wait_recv()
-            for p, (k, l) in enumerate(planes):
+            if arrive:
+                copies[3].wait_recv()
+            for p, k, l in chosen:
                 dst[k, l, 0:1, :] += rows_south[step, p : p + 1, :]
 
     def regrid(step, dst, e):
@@ -249,18 +253,24 @@
             for k in range(comp):
                 dst[k, 0, where, :] = total[k]
 
+    deep = range(1, lev)
     for step, (src, dst) in enumerate(((adjoint, field), (field, out))):
         send_lists(step, src)
         if step == 0:
             coefficients()
+        else:
+            rims(step - 1, src, deep, False)
         inner(step, src, dst)
         if step == 0:
             loads[7].wait()
             loads[8].wait()
         regrid(step, dst, 1)
-        rims(step, dst)
+        regrid(step, dst, 2)
+        if step == STEPS - 1:
+            rims(step, dst, range(lev), True)
         regrid(step, dst, 0)
-        regrid(step, dst, 2)
+        if step < STEPS - 1:
+            rims(step, dst, (0,), True)
 
     for step in range(STEPS):
         for d in range(3):

time: 16.9 us -> 14.8 us (0.88)
  Pallas kernels: 16 us -> 13.9 us
    pallas_call x1, Pallas kernels: 16 us -> 13.9 us  [on_device(): pl.pallas_call(functools.partial(kernel, n_lat, n_lon), out_shape=jax.Sha...]
where the time goes in v5:
time: 14.8 us; the launch traced here: 14.6 us
  Pallas kernels  13.9 us (94%)
  local copies, waits for them, and re-layouts  0.71 us (5%)
    pallas_call x1, Pallas kernels, on_device(): pl.pallas_call(functools.partial(kernel, n_lat, n_lon), out_shape=jax.Sha...  13.9 us
    unnamed x1, local copies, waits for them, and re-layouts  0.71 us

profile of v5, /device:TPU:0, one launch (start us, length us, event | category | flops | bytes accessed | tf_op | source)
XLA Modules:
  0.0 14.6 jit_solution(2547393066433387789)
XLA Ops:
  0.0 13.9 %shard_map.91 = f32[4,4,32,128]{3,2,1,0:T(8,128)S(1)} custom-call(f32[4,4,32,128]{3,2,1,0:T(8,128)} %bitcast.11, f32[4,32,128]{2,1,0:T(8,128)} %bitcast.13, f32[2,4,32,128]{3,2,1,0:T(8,128)} %bitcast.12, f32[4,4]{1,0:T(4,128)} %bitcast.19, s32[32,128]{1,0:T(8,128)} %bitcast.16, s32[32,128]{1,0:T(8,128)} %bitcast.17, s32[3,8,128]{2,1,0:T(8,128)} %bitcast.18, ...), custom_call_target="tpu_custom_call" | custom-call | flops 4000000 | bytes 900000 | tf_op jit(solution)/shard_map/pallas_call | solution.py:297
  13.9 0.7 %copy.11 = f32[1,4,4,32,128]{4,3,2,1,0:T(8,128)} copy(f32[1,4,4,32,128]{4,3,2,1,0:T(8,128)S(1)} %bitcast.10) | data formatting | bytes 524288

commit v6 on v5

--- a/solution.py
+++ b/solution.py
@@ -153,6 +153,7 @@
             coef[2, l] = spread + half_y
             coef[3, l] = spread - half_y
             coef[4, l] = 1.0 - 4.0 * spread
+            coef[5, l] = jnp.where(lane == 0, spread + half_x, spread - half_x)
 
     def send_lists(step, src):
         for k in range(comp):
@@ -178,17 +179,30 @@
                 )
             list_copy(step, d).start()
 
-    def inner(step, src, dst):
+    def send_rims(step, src):
         packed = jnp.zeros((tlat, tlon), jnp.float32)
         for p, (k, l) in enumerate(planes):
             value = src[k, l]
+            rim = coef[5, l] * value
+            turned = pltpu.roll(rim, (2 * p + 2) % tlon, 1)
+            packed = jnp.where((lane + 1) >> 1 == p + 1, turned, packed)
+            rows_first[step, p : p + 1, :] = coef[2, l, 0:1, :] * src[k, l, 0:1, :]
+            rows_last[step, p : p + 1, :] = (
+                coef[3, l, tlat - 1 : tlat, :] * src[k, l, tlat - 1 : tlat, :]
+            )
+        cols_out[step] = packed
+        copies = halo_copies(step)
+        copies[0].start()
+        copies[1].start()
+        pl.when(has_south)(copies[2].start)
+        pl.when(has_north)(copies[3].start)
+
+    def inner(src, dst):
+        for k, l in planes:
+            value = src[k, l]
             to_west = pltpu.roll(coef[0, l] * value, tlon - 1, 1)
             to_east = pltpu.roll(coef[1, l] * value, 1, 1)
-            rim = jnp.where(lane == tlon - 1, to_west, to_east)
-            packed = jnp.where(lane >> 1 == p, pltpu.roll(rim, 2 * p + 1, 1), packed)
             to_south, to_north = coef[2, l] * value, coef[3, l] * value
-            rows_first[step, p : p + 1, :] = to_south[0:1]
-            rows_last[step, p : p + 1, :] = to_north[tlat - 1 : tlat]
             dst[k, l] = (
                 coef[4, l] * value
                 + jnp.where(lane == tlon - 1, 0.0, to_west)
@@ -196,19 +210,14 @@
                 + jnp.where(line == tlat - 1, 0.0, pltpu.roll(to_south, tlat - 1, 0))
                 + jnp.where(line == 0, 0.0, pltpu.roll(to_north, 1, 0))
             )
-        cols_out[step] = packed
-        copies = halo_copies(step)
-        copies[0].start()
-        copies[1].start()
-        pl.when(has_south)(copies[2].start)
-        pl.when(has_north)(copies[3].start)
 
     def rims(step, dst, levels, arrive):
         copies = halo_copies(step)
         if arrive:
             copies[0].wait_recv()
             copies[1].wait_recv()
-        both = jnp.where(lane & 1 == 0, cols_east[step], cols_west[step])
+        from_east = pltpu.roll(cols_east[step], tlon - 2, 1)
+        both = jnp.where(lane & 1 == 0, from_east, cols_west[step])
         edge = (lane == 0) | (lane == tlon - 1)
         chosen = [(p, k, l) for p, (k, l) in enumerate(planes) if l in levels]
         for p, k, l in chosen:
@@ -260,7 +269,8 @@
             coefficients()
         else:
             rims(step - 1, src, deep, False)
-        inner(step, src, dst)
+        send_rims(step, src)
+        inner(src, dst)
         if step == 0:
             loads[7].wait()
             loads[8].wait()
@@ -302,7 +312,7 @@
         scratch_shapes=[
             *(space(array.shape, array.dtype) for space, array in zip(spaces, arrays)),
             pltpu.VMEM(adjoint.shape, f32),
-            pltpu.VMEM((5, lev, tlat, tlon), f32),
+            pltpu.VMEM((6, lev, tlat, tlon), f32),
             pltpu.VMEM((tlat, tlon), f32),
             pltpu.VMEM((comp, tlat, tlon), f32),
             pltpu.VMEM((comp, blocks, ROWS, LANES), f32),

time: 14.8 us -> 14.7 us (level)
  no operation moved by 1% of the time
where the time goes in v6:
time: 14.7 us; the launch traced here: 14.5 us
  Pallas kernels  13.8 us (94%)
  local copies, waits for them, and re-layouts  0.71 us (5%)
    pallas_call x1, Pallas kernels, on_device(): pl.pallas_call(functools.partial(kernel, n_lat, n_lon), out_shape=jax.Sha...  13.8 us
    unnamed x1, local copies, waits for them, and re-layouts  0.71 us

profile of v6, /device:TPU:0, one launch (start us, length us, event | category | flops | bytes accessed | tf_op | source)
XLA Modules:
  0.0 14.5 jit_solution(17170555349084823450)
XLA Ops:
  0.0 13.8 %shard_map.91 = f32[4,4,32,128]{3,2,1,0:T(8,128)S(1)} custom-call(f32[4,4,32,128]{3,2,1,0:T(8,128)} %bitcast.11, f32[4,32,128]{2,1,0:T(8,128)} %bitcast.13, f32[2,4,32,128]{3,2,1,0:T(8,128)} %bitcast.12, f32[4,4]{1,0:T(4,128)} %bitcast.19, s32[32,128]{1,0:T(8,128)} %bitcast.16, s32[32,128]{1,0:T(8,128)} %bitcast.17, s32[3,8,128]{2,1,0:T(8,128)} %bitcast.18, ...), custom_call_target="tpu_custom_call" | custom-call | flops 4000000 | bytes 900000 | tf_op jit(solution)/shard_map/pallas_call | solution.py:307
  13.8 0.7 %copy.11 = f32[1,4,4,32,128]{4,3,2,1,0:T(8,128)} copy(f32[1,4,4,32,128]{4,3,2,1,0:T(8,128)S(1)} %bitcast.10) | data formatting | bytes 524288
